TPU v7x, 512 devices: a whole 4x8x8 slice. The times are simulated.
512 devices in a mesh: wide: 64 (over x, z_hi, y), narrow: 8 (over z_lo, core).
Axes of the slice: x: 4, y: 8, z: 8 (z_hi: 2, z_lo: 4; z = z_hi * 4 + z_lo), core: 2. Of those that a mesh axis runs over, the one named last changes fastest.
Arguments:
- amplitudes: float32 [1024, 16384], P('wide', 'narrow'), may hold values from -6 to 6
- integrals: float32 [16384, 16384], P('narrow', 'wide'), may hold values from -0.125 to 0.125
- residual_in: float32 [1024, 16384], P('narrow', 'wide'), may hold values from -6 to 6
- row_irrep: int32 [1024], P('wide'), may hold values from 0 to 7
- cd_sizes: int32 [8], replicated, may hold values from 1 to 4096, 16384 in all
Outputs:
- ladder_residual: float32 [1024, 16384], P('narrow', 'wide')
Inputs may be any that keep to these rules, and one draw needn't show every extreme that they name: `cd_sizes`: sums to 16384; the largest is exactly 4096.
All inputs are finite; a program needn't handle non-finite values.
Results may differ from a plain program's by a relative error of at most 0.00005.
Values sent between devices are 32-bit elements; how exact they have to be, the bound alone decides.
A program may use at most 64 MiB of HBM per device.

v0:
```python
import jax
import jax.numpy as jnp
from jax import lax
from jax.sharding import PartitionSpec as P


def body(amplitudes, integrals, residual_in, row_irrep, cd_sizes):
    pair_local = amplitudes.shape[1]
    first = lax.axis_index("narrow") * pair_local
    ends = jnp.cumsum(cd_sizes)
    column = first + jnp.arange(pair_local, dtype=jnp.int32)
    col_irrep = jnp.sum((column[:, None] >= ends[None, :]).astype(jnp.int32), axis=1)
    masked = jnp.where(
        row_irrep[:, None] == col_irrep[None, :], amplitudes, jnp.zeros((), amplitudes.dtype)
    )
    partial_sum = jnp.dot(
        lax.all_gather(masked, "wide", axis=0, tiled=True),
        integrals,
        precision=lax.Precision.HIGHEST,
        preferred_element_type=jnp.float32,
    )
    ladder = lax.psum_scatter(partial_sum, "narrow", scatter_dimension=0, tiled=True)
    return residual_in + 0.5 * ladder


def solution(mesh):
    in_specs = (P("wide", "narrow"), P("narrow", "wide"), P("narrow", "wide"), P("wide"), P())
    out_specs = P("narrow", "wide")
    return jax.shard_map(body, mesh=mesh, in_specs=in_specs, out_specs=out_specs, check_vma=False)
```

profile of v0, /device:TPU:1, one launch (start us, length us, event | category | flops | bytes accessed | tf_op | source)
XLA Modules:
  0.0 268.7 jit_solution(5333994218209577182)
XLA Ops:
  6.5 0.0 copy-start
  6.5 0.0 all-gather.2.cloned.1.call-start
  6.5 1.0 reduce-window.8
  7.5 0.1 convert_reduce_fusion
  7.6 1.6 compare_select_fusion
  9.3 0.0 all-gather.2.cloned.1.call-update
  9.3 0.0 copy-start.1
  9.3 0.0 reduce-scatter.2.cloned.1.call-start
  9.3 205.9 %all-gather.2.cloned.1.call-done = f32[1024,2048]{1,0:T(8,128)} async-done(((f32[16,2048]{1,0:T(8,128)}), f32[1024,2048]{1,0:T(8,128)}) %all-gather.2.cloned.1.call-update) | async-done | bytes 8388624 | tf_op jit(solution)/shard_map/all_gather | solution.py:17
  215.3 0.0 copy-done
  215.3 9.9 %fusion = f32[1024,256]{1,0:T(8,128)} fusion(f32[1024,2048]{1,0:T(8,128)} %all-gather.2.cloned.1.call-done, f32[2048,256]{1,0:T(8,128)S(1)} %copy-done), kind=kOutput, calls=%fused_computation.4 | convolution fusion | flops 6442450944 | bytes 11534336 | tf_op jit(solution)/shard_map/dot_general | solution.py:16
  225.2 0.0 reduce-scatter.2.cloned.1.call-update
  225.2 35.0 %reduce-scatter.2.cloned.1.call-done = f32[128,256]{1,0:T(8,128)} async-done(((f32[1024,256]{1,0:T(8,128)}), f32[128,256]{1,0:T(8,128)}) %reduce-scatter.2.cloned.1.call-update) | async-done | bytes 131088 | tf_op jit(solution)/shard_map/reduce_scatter | solution.py:22
  260.3 0.0 copy-done.1
  260.3 1.6 multiply_add_fusion
  (1 shorter events, 0.0 us)
Async XLA Ops:
  6.5 208.7 %copy-start = (f32[2048,256]{1,0:T(8,128)S(1)}, f32[2048,256]{1,0:T(8,128)}, u32[]{:S(2)}) copy-start(f32[2048,256]{1,0:T(8,128)} %param.6) | copy-start | bytes 6291460
  6.5 208.7 %all-gather.2.cloned.1.call-start = ((), (), s32[]{:S(2)}) async-start(), calls=%async_computation.1 | async-start | bytes 8519680 | tf_op jit(solution)/shard_map/all_gather | solution.py:17
  9.3 251.0 %copy-start.1 = (f32[128,256]{1,0:T(8,128)S(1)}, f32[128,256]{1,0:T(8,128)}, u32[]{:S(2)}) copy-start(f32[128,256]{1,0:T(8,128)} %param.7) | copy-start | bytes 393220
  9.3 251.0 %reduce-scatter.2.cloned.1.call-start = ((), (), s32[]{:S(2)}) async-start(), calls=%async_computation.2 | async-start | bytes 1179648 | tf_op jit(solution)/shard_map/reduce_scatter | solution.py:22
Sparse Core Ops, SparseCore 0:
  11.9 203.3 all-gather.1
  225.3 34.8 reduce-scatter.1
where the time goes:
time: 271 us; the launch traced here: 269 us
  waiting for transfers between devices  241 us (89%)
  between operations  13.4 us (5%)
  matrix products  9.94 us (4%)
  other arithmetic  4.29 us (2%)
    all_gather x1, waiting for transfers between devices, body(): lax.all_gather(masked, 'wide', axis=0, tiled=True)  206 us
    reduce_scatter x1, waiting for transfers between devices, body(): lax.psum_scatter(partial_sum, 'narrow', scatter_dimension=0, tiled=True)  35 us
    dot_general x1, matrix products, body(): jnp.dot(lax.all_gather(masked, 'wide', axis=0, tiled=True), integrals, pr...  9.94 us
  transfers between devices with their start and end apart: 2, of which 2 were waited for; matrix products, arithmetic and copies ran while one was open for 0% of the time, Pallas kernels for 0%

commit v1 on v0

v1 whole, which is shorter than its diff:
```python
import functools

import jax
import jax.numpy as jnp
from jax import lax
from jax.experimental import pallas as pl
from jax.experimental.pallas import tpu as pltpu
from jax.sharding import PartitionSpec as P

MESH = pl.DeviceIdType.MESH
F32 = jnp.float32
BF16 = jnp.bfloat16

NX, NZH, NY, NZL, NC = 4, 2, 8, 4, 2
RW = 16
RB = RW * NY
CH = 256
AB = 256
SLOTS = 32
CAP = SLOTS - 1
HALF = SLOTS // 2
NIRR = 8


def split(value):
    high = value.astype(BF16)
    return high, (value - high.astype(F32)).astype(BF16)


def dot(a, b):
    return jnp.dot(a, b, preferred_element_type=F32)


def kernel(
    a_ref, int_ref, res_ref, irr_ref, sizes_ref, off_ref,
    out_ref, cnt_ref,
    int_hi, int_lo, ci_ref, irr_row, raw, raw_irr, qbuf, pbuf, sel, irr_col, ranks, acc, pair, zbuf,
    raw_s, raw_r, ri_s, ri_r, qy_s, qy_r, qx_s, qx_r, py_s, py_r, px_s, px_r, pair_s, pair_r, z_s, z_r,
):
    w, n = lax.axis_index("wide"), lax.axis_index("narrow")
    x, zh, y = w // (NZH * NY), (w // NY) % NZH, w % NY
    zl, c = n // NC, n % NC

    def dev(x_, zh_, y_, zl_, c_):
        return (x_ * (NZH * NY) + zh_ * NY + y_, zl_ * NC + c_)

    ymod = lambda k: lax.rem(y + (k + NY), NY)
    xmod = lambda k: lax.rem(x + (k + NX), NX)
    partner = dev(x, zh, y, zl, 1 - c)
    up, down = dev(x, zh, ymod(1), zl, c), dev(x, zh, ymod(-1), zl, c)
    y_peers = [dev(x, zh, ymod(k), zl, c) for k in range(1, NY)]
    o_peers = [dev(x, 1 - zh, ymod(k), zl, c) for k in range(NY)]
    x_peers = [dev(xmod(k), zh, y, zl, c) for k in range(1, NX)]
    z_peers = [dev(x, zh, y, lax.rem(zl + k, NZL), c) for k in range(1, NZL)]

    barrier = pltpu.get_barrier_semaphore()
    everyone = y_peers + o_peers + x_peers + z_peers + [partner]
    for peer in everyone:
        pl.semaphore_signal(barrier, inc=1, device_id=peer, device_id_type=MESH)

    lane = lax.broadcasted_iota(jnp.int32, (8, 128), 1)
    row = jnp.zeros((8, 128), F32)
    for r in range(RW):
        row = jnp.where(lane == y * RW + r, irr_ref[r].astype(F32), row)
    irr_row[...] = row
    cd = (
        n * (NY * CH)
        + CH * lax.broadcasted_iota(jnp.int32, (NY, CH), 0)
        + lax.broadcasted_iota(jnp.int32, (NY, CH), 1)
    )
    end = jnp.int32(0)
    col = jnp.zeros((NY, CH), F32)
    for i in range(NIRR):
        end = end + sizes_ref[i]
        col = col + jnp.where(cd >= end, 1.0, 0.0)
    ci_ref[...] = col
    off = off_ref[0]

    sends = []

    def send(src, dst, s, r, to):
        copy = pltpu.make_async_remote_copy(
            src_ref=src, dst_ref=dst, send_sem=s, recv_sem=r, device_id=to, device_id_type=MESH
        )
        copy.start()
        return copy

    def arrived(dst, r):
        pltpu.make_async_remote_copy(
            src_ref=dst, dst_ref=dst, send_sem=r, recv_sem=r, device_id=partner, device_id_type=MESH
        ).wait_recv()

    chunk = lambda j: pl.ds(pl.multiple_of(j * CH, CH), CH)

    def split_integrals(j, _):
        high, low = split(int_ref[chunk(j), :])
        int_hi[j] = high
        int_lo[j] = low
        return 0

    pl.semaphore_wait(barrier, len(everyone))

    for k in range(1, NY):
        to = y_peers[k - 1]
        sends.append(send(irr_row.at[pl.ds(0, 1)], raw_irr.at[0, pl.ds(y, 1)], ri_s.at[0, k], ri_r.at[0, k], to))
        sends.append(send(a_ref.at[:, chunk(ymod(k))], raw.at[0, y], raw_s.at[0, k], raw_r.at[0, k], to))
    for k in range(NY):
        to = o_peers[k]
        sends.append(send(irr_row.at[pl.ds(0, 1)], raw_irr.at[1, pl.ds(y, 1)], ri_s.at[1, k], ri_r.at[1, k], to))
        sends.append(send(a_ref.at[:, chunk(ymod(k))], raw.at[1, y], raw_s.at[1, k], raw_r.at[1, k], to))
    raw[0, y] = a_ref[:, chunk(y)]
    raw_irr[0, pl.ds(y, 1)] = row[0:1]
    lax.fori_loop(0, NY, split_integrals, 0)

    sub_i = lax.broadcasted_iota(jnp.int32, (RB, RB), 0)
    lane_i = lax.broadcasted_iota(jnp.int32, (RB, RB), 1)

    def ranks_of(irr_lane):
        along_lane = jnp.broadcast_to(irr_lane, (RB, RB))
        along_sub = along_lane.T
        same = along_lane == along_sub
        rank_lane = jnp.sum(jnp.where(same & (sub_i < lane_i), 1.0, 0.0), axis=0, keepdims=True)
        rank_sub = jnp.sum(jnp.where(same & (lane_i < sub_i), 1.0, 0.0), axis=1, keepdims=True)
        return along_sub, rank_lane, rank_sub

    def pack(group, dst):
        irr_lane = jnp.sum(raw_irr[group], axis=0, keepdims=True)
        along_sub, rank_lane, _ = ranks_of(irr_lane)
        slot = lax.broadcasted_iota(jnp.int32, (SLOTS, RB), 0).astype(F32)
        pick = jnp.where((rank_lane - off == slot) & (slot < CAP), 1.0, 0.0).astype(BF16)
        here = ci_ref[pl.ds(y, 1), :]
        keep = jnp.concatenate([along_sub, along_sub], axis=1) == here
        masked = jnp.where(keep, raw[group].reshape(RB, CH), 0.0)
        high = masked.astype(BF16)
        rest = masked - high.astype(F32)
        mid, low = split(rest)
        packed = dot(pick, high) + dot(pick, mid) + dot(pick, low)
        last = lax.broadcasted_iota(jnp.int32, (SLOTS, CH), 0) == CAP
        tail = jnp.concatenate([irr_lane, jnp.zeros((1, CH - RB), F32)], axis=1)
        dst[...] = jnp.where(last, jnp.broadcast_to(tail, (SLOTS, CH)), packed)

    def open_block(b, src):
        irr_lane = src[pl.ds(CAP, 1), 0:RB]
        along_sub, rank_lane, rank_sub = ranks_of(irr_lane)
        slot = lax.broadcasted_iota(jnp.int32, (RB, SLOTS), 1).astype(F32)
        sel[b] = jnp.where((rank_sub - off == slot) & (slot < CAP), 1.0, 0.0).astype(BF16)
        irr_col[b] = along_sub
        ranks[pl.ds(b, 1), :] = rank_lane

    def multiply(b, src, j):
        high, low = split(src[...])
        pick = sel[b]
        keep = jnp.concatenate([irr_col[b], irr_col[b]], axis=1) == ci_ref[pl.ds(j, 1), :]
        e_hi = jnp.where(keep, dot(pick, high), 0.0).astype(BF16)
        e_lo = jnp.where(keep, dot(pick, low), 0.0).astype(BF16)
        return dot(e_hi, int_hi[j]) + dot(e_lo, int_hi[j]) + dot(e_hi, int_lo[j])

    for k in range(1, NY):
        arrived(raw_irr.at[0, pl.ds(ymod(-k), 1)], ri_r.at[0, k])
        arrived(raw.at[0, ymod(-k)], raw_r.at[0, k])
    pack(0, qbuf.at[x, y])

    def q_along_x(j, slot):
        for k in (1, 3, 2):
            sends.append(send(qbuf.at[x, j], qbuf.at[x, j], qx_s.at[slot, k], qx_r.at[slot, k], x_peers[k - 1]))

    def part(ref, half):
        return ref if half is None else ref.at[pl.ds(half * HALF, HALF)]

    def q_along_y(j, s, direction):
        half = direction if s == NY // 2 else None
        ref = part(qbuf.at[x, j], half)
        sends.append(send(ref, ref, qy_s.at[direction, s], qy_r.at[direction, s], (up, down)[direction]))

    def p_along_y(j, k, s, direction):
        half = direction if s == NY // 2 else None
        ref = part(pbuf.at[j, xmod(-k)], half)
        sends.append(send(ref, ref, py_s.at[direction, s, k], py_r.at[direction, s, k], (up, down)[direction]))

    def q_step(s):
        for direction, j in ((0, ymod(-s)), (1, ymod(s))):
            arrived(qbuf.at[x, j], qy_r.at[direction, s])
            q_along_y(j, s + 1, direction)
            q_along_x(j, 2 * s - 1 + direction)

    def p_step(s, ks):
        for k in ks:
            for direction, j in ((0, ymod(-s)), (1, ymod(s))):
                arrived(pbuf.at[j, xmod(-k)], py_r.at[direction, s, k])
                p_along_y(j, k, s + 1, direction)

    q_along_y(y, 1, 0)
    q_along_y(y, 1, 1)
    q_along_x(y, 0)

    for k in range(NY):
        arrived(raw_irr.at[1, pl.ds(ymod(-k), 1)], ri_r.at[1, k])
        arrived(raw.at[1, ymod(-k)], raw_r.at[1, k])
    pack(1, pbuf.at[y, x])
    p_along_y(y, 0, 1, 0)
    p_along_y(y, 0, 1, 1)
    for k in (1, 3, 2):
        sends.append(send(pbuf.at[y, x], pbuf.at[y, x], px_s.at[k], px_r.at[k], x_peers[k - 1]))

    q_step(1)
    for k in (1, 3, 2):
        arrived(pbuf.at[y, xmod(-k)], px_r.at[k])
        p_along_y(y, k, 1, 0)
        p_along_y(y, k, 1, 1)
    q_step(2)
    p_step(1, (0, 1, 3, 2))
    for k in range(NX):
        open_block(NX + k, pbuf.at[y, k])

    def p_multiply(j, first=False):
        def one(k, _):
            term = multiply(NX + k, pbuf.at[j, k], j)
            if first:
                acc[NX + k] = term
            else:
                acc[NX + k] += term
            return 0

        lax.fori_loop(0, NX, one, 0)

    p_multiply(y, first=True)
    q_step(3)
    for k in range(1, NX):
        arrived(qbuf.at[xmod(-k), y], qx_r.at[0, k])
    p_step(2, (0, 1, 3, 2))
    for k in range(NX):
        open_block(k, qbuf.at[k, y])
    p_multiply(ymod(-1))
    p_multiply(ymod(1))
    opposite = ymod(NY // 2)
    for direction in (0, 1):
        arrived(part(qbuf.at[x, opposite], direction), qy_r.at[direction, NY // 2])
    q_along_x(opposite, NY - 1)
    p_step(3, (0, 1, 3, 2))
    p_multiply(ymod(-2))
    p_multiply(ymod(2))

    for s in range(1, NY // 2):
        for k in range(1, NX):
            arrived(qbuf.at[xmod(-k), ymod(-s)], qx_r.at[2 * s - 1, k])
            arrived(qbuf.at[xmod(-k), ymod(s)], qx_r.at[2 * s, k])
    for k in range(1, NX):
        arrived(qbuf.at[xmod(-k), opposite], qx_r.at[NY - 1, k])

    def pair_copy(base, d):
        return pltpu.make_async_remote_copy(
            src_ref=acc.at[base + d], dst_ref=pair.at[d], send_sem=pair_s.at[d], recv_sem=pair_r.at[d],
            device_id=partner, device_id_type=MESH,
        )

    def z_copy(base, d):
        slot = lax.rem(zl - d + NZL, NZL)
        return pltpu.make_async_remote_copy(
            src_ref=acc.at[base + d], dst_ref=zbuf.at[slot], send_sem=z_s.at[d], recv_sem=z_r.at[slot],
            device_id=dev(x, zh, y, d, c), device_id_type=MESH,
        )

    def nth(t):
        return jnp.where(zl < NZL // 2, NZL - 1 - t, t)

    def give(base):
        def one(t, _):
            pair_copy(base, nth(t)).start()
            return 0

        lax.fori_loop(0, NZL, one, 0)

    def take(base):
        def one(t, _):
            d = nth(t)
            arrived(pair.at[d], pair_r.at[d])
            acc[base + d] += pair[d]

            @pl.when(d != zl)
            def _():
                z_copy(base, d).start()

            return 0

        lax.fori_loop(0, NZL, one, 0)

    def finish(base):
        total = acc[base + zl]
        for k in range(1, NZL):
            arrived(zbuf.at[k], z_r.at[k])
            total = total + zbuf[k]
        out_ref[...] = res_ref[...] + 0.5 * total

        def one(d, _):
            @pl.when(d != zl)
            def _():
                z_copy(base, d).wait_send()

            return 0

        lax.fori_loop(0, NZL, one, 0)

    keeps_q = c == zh

    def q_multiply(k, _):
        def one(j, _):
            acc[k] += multiply(k, qbuf.at[k, j], j)
            return 0

        acc[k] = multiply(k, qbuf.at[k, 0], 0)
        lax.fori_loop(1, NY, one, 0)
        return 0

    lax.fori_loop(0, NX, q_multiply, 0)

    @pl.when(jnp.logical_not(keeps_q))
    def _():
        give(0)

    @pl.when(keeps_q)
    def _():
        take(0)

    p_multiply(ymod(-3))
    p_multiply(ymod(3))
    for k in (0, 1, 3, 2):
        for direction in (0, 1):
            arrived(part(pbuf.at[opposite, xmod(-k)], direction), py_r.at[direction, NY // 2, k])
    p_multiply(opposite)

    @pl.when(keeps_q)
    def _():
        give(NX)
        finish(0)
        for d in range(NZL):
            pair_copy(NX, d).wait_send()

    @pl.when(jnp.logical_not(keeps_q))
    def _():
        take(NX)
        finish(NX)
        for d in range(NZL):
            pair_copy(0, d).wait_send()

    cnt_ref[0] = jnp.max(ranks[...])
    for copy in sends:
        copy.wait_send()


def one_pass(amplitudes, integrals, start, row_irrep, cd_sizes, off):
    dma = pltpu.SemaphoreType.DMA
    vmem, smem = pl.BlockSpec(memory_space=pltpu.VMEM), pl.BlockSpec(memory_space=pltpu.SMEM)
    return pl.pallas_call(
        kernel,
        out_shape=(jax.ShapeDtypeStruct((RB, AB), F32), jax.ShapeDtypeStruct((1,), F32)),
        in_specs=[vmem, vmem, vmem, smem, smem, smem],
        out_specs=(vmem, smem),
        scratch_shapes=[
            pltpu.VMEM((NY, CH, AB), BF16),
            pltpu.VMEM((NY, CH, AB), BF16),
            pltpu.VMEM((NY, CH), F32),
            pltpu.VMEM((8, RB), F32),
            pltpu.VMEM((2, NY, RW, CH), F32),
            pltpu.VMEM((2, NY, RB), F32),
            pltpu.VMEM((NX, NY, SLOTS, CH), F32),
            pltpu.VMEM((NY, NX, SLOTS, CH), F32),
            pltpu.VMEM((2 * NX, RB, SLOTS), BF16),
            pltpu.VMEM((2 * NX, RB, RB), F32),
            pltpu.VMEM((2 * NX, RB), F32),
            pltpu.VMEM((2 * NX, RB, AB), F32),
            pltpu.VMEM((NZL, RB, AB), F32),
            pltpu.VMEM((NZL, RB, AB), F32),
            dma((2, NY)), dma((2, NY)), dma((2, NY)), dma((2, NY)),
            dma((2, 5)), dma((2, 5)), dma((NY, NX)), dma((NY, NX)),
            dma((2, 5, NX)), dma((2, 5, NX)), dma((NX,)), dma((NX,)),
            dma((NZL,)), dma((NZL,)), dma((NZL,)), dma((NZL,)),
        ],
        compiler_params=pltpu.CompilerParams(
            collective_id=0, has_side_effects=True, vmem_limit_bytes=40 * 2**20
        ),
        name="ladder",
    )(amplitudes, integrals, start, row_irrep, cd_sizes, off)


def body(amplitudes, integrals, residual_in, row_irrep, cd_sizes):
    def run(start, off):
        return one_pass(amplitudes, integrals, start, row_irrep, cd_sizes, off)

    def more(state):
        _, top, off = state
        return top[0] >= off[0]

    def again(state):
        total, _, off = state
        total, top = run(total, off)
        return total, top, off + CAP

    zero = jnp.zeros((1,), F32)
    total, top = run(residual_in, zero)
    return lax.while_loop(more, again, (total, top, zero + CAP))[0]


def solution(mesh):
    in_specs = (P("wide", "narrow"), P("narrow", "wide"), P("narrow", "wide"), P("wide"), P())
    out_specs = P("narrow", "wide")
    return jax.shard_map(body, mesh=mesh, in_specs=in_specs, out_specs=out_specs, check_vma=False)
```

time: 271 us -> 75.3 us (0.28)
  waiting for transfers between devices: 241 us -> 0 us
  Pallas kernels: 0 us -> 72.8 us
  between operations: 13.4 us -> 0.05 us
  matrix products: 9.94 us -> 0 us
  other arithmetic: 4.29 us -> 0 us
    all_gather x1 -> x0, waiting for transfers between devices: 206 us -> none  [body(): lax.all_gather(masked, 'wide', axis=0, tiled=True)]
    pallas_call x0 -> x1, Pallas kernels: none -> 72.8 us  [one_pass(): pl.pallas_call(kernel, out_shape=(jax.ShapeDtypeStruct((RB, AB), F32), ja...]
    reduce_scatter x1 -> x0, waiting for transfers between devices: 35 us -> none  [body(): lax.psum_scatter(partial_sum, 'narrow', scatter_dimension=0, tiled=True)]
    dot_general x1 -> x0, matrix products: 9.94 us -> none  [body(): jnp.dot(lax.all_gather(masked, 'wide', axis=0, tiled=True), integrals, pr...]
  transfers between devices with their start and end apart: 2 -> 0, of which waited for: 2 -> 0; matrix products, arithmetic and copies ran while one was open for 0% -> 0% of each run, Pallas kernels for 0% -> 0%
where the time goes in v1:
time: 75.3 us; the launch traced here: 75.2 us
  Pallas kernels  72.8 us (97%)
  local copies, waits for them, and re-layouts  1.6 us (2%)
    pallas_call x1, Pallas kernels, one_pass(): pl.pallas_call(kernel, out_shape=(jax.ShapeDtypeStruct((RB, AB), F32), ja...  72.8 us
    unnamed x11, local copies, waits for them, and re-layouts  1.6 us

profile of v1, /device:TPU:1, one launch (start us, length us, event | category | flops | bytes accessed | tf_op | source)
XLA Modules:
  0.0 75.2 jit_solution(12356245016397884550)
XLA Ops:
  0.0 0.0 copy-start.4
  0.0 0.0 copy-start.3
  0.0 0.0 copy-start
  0.0 0.9 %copy-done = f32[128,256]{1,0:T(8,128)S(1)} copy-done((f32[128,256]{1,0:T(8,128)S(1)}, f32[128,256]{1,0:T(8,128)}, u32[]{:S(2)}) %copy-start) | copy-done | bytes 131096
  0.9 0.0 copy-start.1
  0.9 0.0 copy-start.2
  0.9 72.8 %ladder.2 = (f32[128,256]{1,0:T(8,128)S(1)}, f32[1]{0:T(128)}) custom-call(f32[16,2048]{1,0:T(8,128)} %a_ref.1, f32[2048,256]{1,0:T(8,128)} %int_ref.1, f32[128,256]{1,0:T(8,128)S(1)} %copy-done, s32[16]{0:T(128)} %irr_ref.1, s32[8]{0:T(128)} %sizes_ref.1, f32[1]{0:T(128)} %constant.1.clone.1.off_ref), custom_call_target="tpu_custom_call" | custom-call | tf_op jit(solution)/shard_map/ladder/pallas_call | solution.py:353
  73.8 0.0 copy-done.4
  73.8 0.0 copy-done.3
  73.8 0.0 copy-done.1
  73.8 0.0 copy-done.2
  73.8 0.7 while.12
  74.5 0.7 copy.20
Async XLA Ops:
  0.0 73.8 %copy-start.4 = (s32[8]{0:T(128)S(1)}, s32[8]{0:T(128)}, u32[]{:S(2)}) copy-start(s32[8]{0:T(128)} %sizes_ref.1) | copy-start | bytes 100
  0.0 73.8 %copy-start.3 = (s32[16]{0:T(128)S(1)}, s32[16]{0:T(128)}, u32[]{:S(2)}) copy-start(s32[16]{0:T(128)} %irr_ref.1) | copy-start | bytes 196
  0.0 0.9 %copy-start = (f32[128,256]{1,0:T(8,128)S(1)}, f32[128,256]{1,0:T(8,128)}, u32[]{:S(2)}) copy-start(f32[128,256]{1,0:T(8,128)} %res_ref.1) | copy-start | bytes 393220
  0.9 72.9 %copy-start.1 = (f32[2048,256]{1,0:T(8,128)S(1)}, f32[2048,256]{1,0:T(8,128)}, u32[]{:S(2)}) copy-start(f32[2048,256]{1,0:T(8,128)} %int_ref.1) | copy-start | bytes 6291460
  0.9 72.9 %copy-start.2 = (f32[16,2048]{1,0:T(8,128)S(1)}, f32[16,2048]{1,0:T(8,128)}, u32[]{:S(2)}) copy-start(f32[16,2048]{1,0:T(8,128)} %a_ref.1) | copy-start | bytes 393220

commit v2 on v1

v2 whole, which is shorter than its diff:
```python
import functools

import jax
import jax.numpy as jnp
from jax import lax
from jax.experimental import pallas as pl
from jax.experimental.pallas import tpu as pltpu
from jax.sharding import PartitionSpec as P

MESH = pl.DeviceIdType.MESH
F32 = jnp.float32
BF16 = jnp.bfloat16

NX, NZH, NY, NZL, NC = 4, 2, 8, 4, 2
RW = 16
RB = RW * NY
CH = 256
AB = 256
SLOTS = 32
CAP = SLOTS - 1
HALF = SLOTS // 2
NIRR = 8


def split(value):
    high = value.astype(BF16)
    return high, (value - high.astype(F32)).astype(BF16)


def dot(a, b):
    return jnp.dot(a, b, preferred_element_type=F32)


def kernel(
    a_hbm, int_hbm, res_hbm, irr_hbm, sizes_hbm, off_hbm,
    out_ref, cnt_ref,
    a_ref, int_ref, res_ref, irr_ref, sizes_ref, off_ref, int3, ci_ref, irr_row, raw, raw_irr, qbuf, pbuf, sel, irr_col, ranks, acc, pair, zbuf,
    in_s, raw_s, raw_r, ri_s, ri_r, qy_s, qy_r, qx_s, qx_r, py_s, py_r, px_s, px_r, zx_s, zx_r,
    pair_s, pair_r, z_s, z_r,
):
    w, n = lax.axis_index("wide"), lax.axis_index("narrow")
    x, zh, y = w // (NZH * NY), (w // NY) % NZH, w % NY
    zl, c = n // NC, n % NC

    def dev(x_, zh_, y_, zl_, c_):
        return (x_ * (NZH * NY) + zh_ * NY + y_, zl_ * NC + c_)

    ymod = lambda k: lax.rem(y + (k + NY), NY)
    xmod = lambda k: lax.rem(x + (k + NX), NX)
    partner = dev(x, zh, y, zl, 1 - c)
    up, down = dev(x, zh, ymod(1), zl, c), dev(x, zh, ymod(-1), zl, c)
    y_peers = [dev(x, zh, ymod(k), zl, c) for k in range(1, NY)]
    across = dev(x, 1 - zh, y, zl, c)
    x_peers = [dev(xmod(k), zh, y, zl, c) for k in range(1, NX)]
    z_peers = [dev(x, zh, y, lax.rem(zl + k, NZL), c) for k in range(1, NZL)]

    barrier = pltpu.get_barrier_semaphore()
    everyone = y_peers + x_peers + z_peers + [partner, across]
    for peer in everyone:
        pl.semaphore_signal(barrier, inc=1, device_id=peer, device_id_type=MESH)

    loads = [
        pltpu.make_async_copy(src, dst, in_s.at[i])
        for i, (src, dst) in enumerate((
            (a_hbm, a_ref), (int_hbm, int_ref), (res_hbm, res_ref),
            (irr_hbm, irr_ref), (sizes_hbm, sizes_ref), (off_hbm, off_ref),
        ))
    ]
    for load in loads:
        load.start()
    for load in loads[3:]:
        load.wait()
    lane = lax.broadcasted_iota(jnp.int32, (8, 128), 1)
    row = jnp.zeros((8, 128), F32)
    for r in range(RW):
        row = jnp.where(lane == y * RW + r, irr_ref[r].astype(F32), row)
    irr_row[...] = row
    cd = (
        n * (NY * CH)
        + CH * lax.broadcasted_iota(jnp.int32, (NY, CH), 0)
        + lax.broadcasted_iota(jnp.int32, (NY, CH), 1)
    )
    end = jnp.int32(0)
    col = jnp.zeros((NY, CH), F32)
    for i in range(NIRR):
        end = end + sizes_ref[i]
        col = col + jnp.where(cd >= end, 1.0, 0.0)
    ci_ref[...] = col
    off = off_ref[0]

    def send(src, dst, s, r, to):
        copy = pltpu.make_async_remote_copy(
            src_ref=src, dst_ref=dst, send_sem=s, recv_sem=r, device_id=to, device_id_type=MESH
        )
        copy.start()

    def sent(total, s):
        pltpu.make_async_remote_copy(
            src_ref=total, dst_ref=total, send_sem=s, recv_sem=s, device_id=partner, device_id_type=MESH
        ).wait_send()

    def arrived(dst, r):
        pltpu.make_async_remote_copy(
            src_ref=dst, dst_ref=dst, send_sem=r, recv_sem=r, device_id=partner, device_id_type=MESH
        ).wait_recv()

    chunk = lambda j: pl.ds(pl.multiple_of(j * CH, CH), CH)

    def split_integrals(j, _):
        high, low = split(int_ref[chunk(j), :])
        int3[j, 0:CH] = high
        int3[j, CH:2 * CH] = high
        int3[j, 2 * CH:] = low
        return 0

    loads[0].wait()
    pl.semaphore_wait(barrier, len(everyone))

    for k in (4, 3, 5, 2, 6, 1, 7):
        to = y_peers[k - 1]
        send(irr_row.at[pl.ds(0, 1)], raw_irr.at[pl.ds(y, 1)], ri_s.at[0], ri_r.at[0], to)
        send(a_ref.at[:, chunk(ymod(k))], raw.at[y], raw_s.at[0], raw_r.at[0], to)
    raw[y] = a_ref[:, chunk(y)]
    raw_irr[pl.ds(y, 1), :] = row[0:1]
    loads[1].wait()
    lax.fori_loop(0, NY, split_integrals, 0)

    sub_i = lax.broadcasted_iota(jnp.int32, (RB, RB), 0)
    lane_i = lax.broadcasted_iota(jnp.int32, (RB, RB), 1)

    def ranks_of(irr_lane):
        along_lane = jnp.broadcast_to(irr_lane, (RB, RB))
        along_sub = along_lane.T
        same = along_lane == along_sub
        rank_lane = jnp.sum(jnp.where(same & (sub_i < lane_i), 1.0, 0.0), axis=0, keepdims=True)
        rank_sub = jnp.sum(jnp.where(same & (lane_i < sub_i), 1.0, 0.0), axis=1, keepdims=True)
        return along_sub, rank_lane, rank_sub

    def pack(dst):
        irr_lane = jnp.sum(raw_irr[...], axis=0, keepdims=True)
        along_sub, rank_lane, _ = ranks_of(irr_lane)
        slot = lax.broadcasted_iota(jnp.int32, (SLOTS, RB), 0).astype(F32)
        pick = jnp.where((rank_lane - off == slot) & (slot < CAP), 1.0, 0.0).astype(BF16)
        here = ci_ref[pl.ds(y, 1), :]
        keep = jnp.concatenate([along_sub, along_sub], axis=1) == here
        masked = jnp.where(keep, raw[...].reshape(RB, CH), 0.0)
        high = masked.astype(BF16)
        rest = masked - high.astype(F32)
        mid, low = split(rest)
        packed = dot(pick, high) + dot(pick, mid) + dot(pick, low)
        last = lax.broadcasted_iota(jnp.int32, (SLOTS, CH), 0) == CAP
        tail = jnp.concatenate([irr_lane, jnp.zeros((1, CH - RB), F32)], axis=1)
        dst[...] = jnp.where(last, jnp.broadcast_to(tail, (SLOTS, CH)), packed)

    def open_blocks(g, srcs):
        for k, src in enumerate(srcs):
            irr_lane = src[pl.ds(CAP, 1), 0:RB]
            along_sub, rank_lane, rank_sub = ranks_of(irr_lane)
            slot = lax.broadcasted_iota(jnp.int32, (RB, NX * SLOTS), 1) - k * SLOTS
            pick = (rank_sub - off == slot.astype(F32)) & (slot >= 0) & (slot < CAP)
            sel[g, k * RB:(k + 1) * RB, :] = jnp.where(pick, 1.0, 0.0).astype(BF16)
            irr_col[g, k * RB:(k + 1) * RB, :] = along_sub
            ranks[pl.ds(NX * g + k, 1), :] = rank_lane

    def multiply(g, src, j, first=False):
        high, low = split(src.reshape(NX * SLOTS, CH))
        spread = dot(sel[g], jnp.concatenate([high, low], axis=1))
        keep = jnp.concatenate([irr_col[g], irr_col[g]], axis=1) == ci_ref[pl.ds(j, 1), :]
        e_hi = jnp.where(keep, spread[:, :CH], 0.0).astype(BF16)
        e_lo = jnp.where(keep, spread[:, CH:], 0.0).astype(BF16)
        term = dot(jnp.concatenate([e_hi, e_lo, e_hi], axis=1), int3[j])
        if first:
            acc[g] = term
        else:
            acc[g] += term

    arrived(raw_irr.at[pl.ds(0, NY - 1)], ri_r.at[0])
    arrived(raw.at[pl.ds(0, NY - 1)], raw_r.at[0])
    pack(qbuf.at[x, y])

    def q_along_x(j, slot):
        for k in (1, 3, 2):
            send(qbuf.at[x, j], qbuf.at[x, j], qx_s.at[0], qx_r.at[slot], x_peers[k - 1])

    def part(ref, half):
        return ref if half is None else ref.at[pl.ds(half * HALF, HALF)]

    def p_along_y(j, k, s, direction):
        half = direction if s == NY // 2 else None
        ref = part(pbuf.at[j, xmod(-k)], half)
        send(ref, ref, py_s.at[0], py_r.at[direction, s, k], (up, down)[direction])

    def q_step(k):
        arrived(qbuf.at[x, ymod(-k)], qy_r.at[k])
        q_along_x(ymod(-k), k)

    def p_step(s, ks):
        for k in ks:
            for direction, j in ((0, ymod(-s)), (1, ymod(s))):
                arrived(pbuf.at[j, xmod(-k)], py_r.at[direction, s, k])
                p_along_y(j, k, s + 1, direction)

    send(qbuf.at[x, y], pbuf.at[y, x], zx_s.at[0], zx_r.at[0], across)
    for k in (1, 7, 2, 6, 3, 5, 4):
        send(qbuf.at[x, y], qbuf.at[x, y], qy_s.at[0], qy_r.at[k], y_peers[k - 1])
    q_along_x(y, 0)

    opposite = ymod(NY // 2)

    def q_multiply(slot, first=False):
        j = ymod(-slot)
        arrived(qbuf.at[0, pl.ds(0, NX - 1)], qx_r.at[slot])
        if first:
            open_blocks(0, [qbuf.at[k, j] for k in range(NX)])
        multiply(0, qbuf[:, j], j, first)

    def p_multiply(j, first=False):
        if first:
            open_blocks(1, [pbuf.at[j, k] for k in range(NX)])
        multiply(1, pbuf[j], j, first)

    for k in (1, 7, 2, 6):
        q_step(k)
    arrived(pbuf.at[y, x], zx_r.at[0])
    p_along_y(y, 0, 1, 0)
    p_along_y(y, 0, 1, 1)
    for k in (1, 3, 2):
        send(pbuf.at[y, x], pbuf.at[y, x], px_s.at[0], px_r.at[k], x_peers[k - 1])
    for k in (3, 5, 4):
        q_step(k)
    q_multiply(0, first=True)
    p_step(1, (0,))
    for k in (1, 3, 2):
        arrived(pbuf.at[y, xmod(-k)], px_r.at[k])
        p_along_y(y, k, 1, 0)
        p_along_y(y, k, 1, 1)
    q_multiply(1)
    q_multiply(7)
    p_step(1, (1, 3, 2))
    p_multiply(y, first=True)
    q_multiply(2)
    q_multiply(6)
    p_step(2, (0,))
    q_multiply(3)
    q_multiply(5)
    p_step(2, (1, 3, 2))
    q_multiply(4)

    block = lambda d: pl.ds(pl.multiple_of(d * RB, RB), RB)

    def pair_copy(g, d):
        return pltpu.make_async_remote_copy(
            src_ref=acc.at[g, block(d)], dst_ref=pair.at[d], send_sem=pair_s.at[0], recv_sem=pair_r.at[d],
            device_id=partner, device_id_type=MESH,
        )

    def z_copy(g, d):
        slot = lax.rem(zl - d + NZL, NZL) - 1
        return pltpu.make_async_remote_copy(
            src_ref=acc.at[g, block(d)], dst_ref=zbuf.at[slot], send_sem=z_s.at[0], recv_sem=z_r.at[0],
            device_id=dev(x, zh, y, d, c), device_id_type=MESH,
        )

    def nth(t):
        return jnp.where(zl < NZL // 2, NZL - 1 - t, t)

    def give(g):
        def one(t, _):
            pair_copy(g, nth(t)).start()
            return 0

        lax.fori_loop(0, NZL, one, 0)

    def take(g):
        def one(t, _):
            d = nth(t)
            arrived(pair.at[d], pair_r.at[d])
            acc[g, block(d)] += pair[d]

            @pl.when(d != zl)
            def _():
                z_copy(g, d).start()

            return 0

        lax.fori_loop(0, NZL, one, 0)

    def finish(g):
        total = acc[g, block(zl)]
        arrived(zbuf.at[pl.ds(0, NZL - 1)], z_r.at[0])
        for k in range(NZL - 1):
            total = total + zbuf[k]
        loads[2].wait()
        out_ref[...] = res_ref[...] + 0.5 * total

    keeps_q = c == zh

    @pl.when(jnp.logical_not(keeps_q))
    def _():
        give(0)

    p_multiply(ymod(-1))
    p_multiply(ymod(1))

    @pl.when(keeps_q)
    def _():
        take(0)

    p_step(3, (0, 1, 3, 2))
    for s in (2, 3):
        p_multiply(ymod(-s))
        p_multiply(ymod(s))
    for k in (0, 1, 3, 2):
        for direction in (0, 1):
            arrived(part(pbuf.at[opposite, xmod(-k)], direction), py_r.at[direction, NY // 2, k])
    p_multiply(opposite)

    @pl.when(keeps_q)
    def _():
        give(1)
        finish(0)

    @pl.when(jnp.logical_not(keeps_q))
    def _():
        take(1)
        finish(1)

    cnt_ref[0] = jnp.max(ranks[...])
    sent(raw.at[pl.ds(0, NY - 1)], raw_s.at[0])
    sent(raw_irr.at[pl.ds(0, NY - 1)], ri_s.at[0])
    sent(qbuf.at[0, 0], zx_s.at[0])
    sent(qbuf.at[0, pl.ds(0, NY - 1)], qy_s.at[0])
    sent(qbuf.at[pl.ds(0, NX - 1)], qx_s.at[0])
    sent(pbuf.at[0, pl.ds(0, NX - 1)], px_s.at[0])
    sent(pbuf.at[pl.ds(0, NY - 1)], py_s.at[0])
    sent(pair, pair_s.at[0])
    sent(zbuf.at[pl.ds(0, NZL - 1)], z_s.at[0])


def one_pass(amplitudes, integrals, start, row_irrep, cd_sizes, off):
    dma = pltpu.SemaphoreType.DMA
    hbm = pl.BlockSpec(memory_space=pltpu.HBM)
    vmem, smem = pl.BlockSpec(memory_space=pltpu.VMEM), pl.BlockSpec(memory_space=pltpu.SMEM)
    return pl.pallas_call(
        kernel,
        out_shape=(jax.ShapeDtypeStruct((RB, AB), F32), jax.ShapeDtypeStruct((1,), F32)),
        in_specs=[hbm] * 6,
        out_specs=(vmem, smem),
        scratch_shapes=[
            pltpu.VMEM((RW, NY * CH), F32),
            pltpu.VMEM((NY * CH, AB), F32),
            pltpu.VMEM((RB, AB), F32),
            pltpu.SMEM((RW,), jnp.int32),
            pltpu.SMEM((NIRR,), jnp.int32),
            pltpu.SMEM((1,), F32),
            pltpu.VMEM((NY, 3 * CH, AB), BF16),
            pltpu.VMEM((NY, CH), F32),
            pltpu.VMEM((8, RB), F32),
            pltpu.VMEM((NY, RW, CH), F32),
            pltpu.VMEM((NY, RB), F32),
            pltpu.VMEM((NX, NY, SLOTS, CH), F32),
            pltpu.VMEM((NY, NX, SLOTS, CH), F32),
            pltpu.VMEM((NZH, NX * RB, NX * SLOTS), BF16),
            pltpu.VMEM((NZH, NX * RB, RB), F32),
            pltpu.VMEM((2 * NX, RB), F32),
            pltpu.VMEM((NZH, NX * RB, AB), F32),
            pltpu.VMEM((NZL, RB, AB), F32),
            pltpu.VMEM((NZL - 1, RB, AB), F32),
            dma((6,)), dma((1,)), dma((1,)), dma((1,)), dma((1,)),
            dma((1,)), dma((NY,)), dma((1,)), dma((NY,)),
            dma((1,)), dma((2, 5, NX)), dma((1,)), dma((NX,)), dma((1,)), dma((1,)),
            dma((1,)), dma((NZL,)), dma((1,)), dma((1,)),
        ],
        compiler_params=pltpu.CompilerParams(
            collective_id=0, has_side_effects=True, vmem_limit_bytes=40 * 2**20
        ),
        name="ladder",
    )(amplitudes, integrals, start, row_irrep, cd_sizes, off)


def body(amplitudes, integrals, residual_in, row_irrep, cd_sizes):
    def run(start, off):
        return one_pass(amplitudes, integrals, start, row_irrep, cd_sizes, off)

    def more(state):
        _, top, off = state
        return top[0] >= off[0]

    def again(state):
        total, _, off = state
        total, top = run(total, off)
        return total, top, off + CAP

    zero = jnp.zeros((1,), F32)
    total, top = run(residual_in, zero)
    return lax.while_loop(more, again, (total, top, zero + CAP))[0]


def solution(mesh):
    in_specs = (P("wide", "narrow"), P("narrow", "wide"), P("narrow", "wide"), P("wide"), P())
    out_specs = P("narrow", "wide")
    return jax.shard_map(body, mesh=mesh, in_specs=in_specs, out_specs=out_specs, check_vma=False)
```

time: 75.3 us -> 109 us (1.45)
  Pallas kernels: 72.8 us -> 106 us
    pallas_call x1 -> x2, Pallas kernels: 72.8 us -> 106 us  [one_pass(): pl.pallas_call(kernel, out_shape=(jax.ShapeDtypeStruct((RB, AB), F32), ja...]
where the time goes in v2:
time: 109 us
  Pallas kernels  106 us (97%)
  local copies, waits for them, and re-layouts  1.61 us (1%)
  loops' own time  1.57 us (1%)
    pallas_call x2, Pallas kernels, one_pass(): pl.pallas_call(kernel, out_shape=(jax.ShapeDtypeStruct((RB, AB), F32), ja...  106 us

profile of v2, /device:TPU:1, one launch (start us, length us, event | category | flops | bytes accessed | tf_op | source)
XLA Modules:
  0.0 109.3 jit_solution(7129990941471245719)
XLA Ops:
  0.0 0.0 copy-start.4
  0.0 0.0 copy-start.3
  0.0 0.0 copy-start
  0.0 0.9 copy-done
  0.9 0.0 copy-start.1
  0.9 0.0 copy-start.2
  0.9 59.0 %ladder.2 = (f32[128,256]{1,0:T(8,128)S(1)}, f32[1]{0:T(128)}) custom-call(f32[16,2048]{1,0:T(8,128)} %a_hbm.1, f32[2048,256]{1,0:T(8,128)} %int_hbm.1, f32[128,256]{1,0:T(8,128)S(1)} %copy-done, s32[16]{0:T(128)} %irr_hbm.1, s32[8]{0:T(128)} %sizes_hbm.1, f32[1]{0:T(128)} %constant.1.clone.1.off_hbm), custom_call_target="tpu_custom_call" | custom-call | tf_op jit(solution)/shard_map/ladder/pallas_call | solution.py:344
  59.9 0.0 copy-done.4
  59.9 0.0 copy-done.3
  59.9 0.0 copy-done.1
  59.9 0.0 copy-done.2
  59.9 48.7 %while.12 = (f32[128,256]{1,0:T(8,128)S(1)}, f32[1]{0:T(128)}, f32[1]{0:T(128)}, f32[16,2048]{1,0:T(8,128)S(1)}, f32[2048,256]{1,0:T(8,128)S(1)}, /*index=5*/s32[16]{0:T(128)S(1)}, s32[8]{0:T(128)S(1)}, f32[1]{0:T(128)}) while((f32[128,256]{1,0:T(8,128)S(1)}, f32[1]{0:T(128)}, f32[1]{0:T(128)}, f32[16,2048]{1,0:T(8,128)S(1)}, ...), condition=%wide.region_1.0_spmd, body=%wide.region_0.0_spmd | while | flops 2 | bytes 262237 | solution.py:396
  60.8 47.1 %ladder.3 = (f32[128,256]{1,0:T(8,128)S(1)}, f32[1]{0:T(128)}) custom-call(f32[16,2048]{1,0:T(8,128)S(1)} %get-tuple-element.120.a_hbm, f32[2048,256]{1,0:T(8,128)S(1)} %get-tuple-element.121.int_hbm, f32[128,256]{1,0:T(8,128)S(1)} %copy.19.res_hbm, s32[16]{0:T(128)S(1)} %get-tuple-element.122.irr_hbm, s32[8]{0:T(128)S(1)} %get-tuple-element.123.sizes_hbm, ...), custom_call_target="tpu_custom_call" | custom-call | tf_op jit(solution)/shard_map/while/body/ladder/pallas_call | solution.py:344
  108.6 0.7 copy.20
  (1 shorter events, 0.0 us)
Async XLA Ops:
  0.0 59.9 %copy-start.4 = (s32[8]{0:T(128)S(1)}, s32[8]{0:T(128)}, u32[]{:S(2)}) copy-start(s32[8]{0:T(128)} %sizes_hbm.1) | copy-start | bytes 100
  0.0 59.9 %copy-start.3 = (s32[16]{0:T(128)S(1)}, s32[16]{0:T(128)}, u32[]{:S(2)}) copy-start(s32[16]{0:T(128)} %irr_hbm.1) | copy-start | bytes 196
  0.0 0.9 copy-start
  0.9 59.0 %copy-start.1 = (f32[2048,256]{1,0:T(8,128)S(1)}, f32[2048,256]{1,0:T(8,128)}, u32[]{:S(2)}) copy-start(f32[2048,256]{1,0:T(8,128)} %int_hbm.1) | copy-start | bytes 6291460
  0.9 59.0 %copy-start.2 = (f32[16,2048]{1,0:T(8,128)S(1)}, f32[16,2048]{1,0:T(8,128)}, u32[]{:S(2)}) copy-start(f32[16,2048]{1,0:T(8,128)} %a_hbm.1) | copy-start | bytes 393220

commit v3 on v2

--- a/solution.py
+++ b/solution.py
@@ -19,6 +19,9 @@
 SLOTS = 32
 CAP = SLOTS - 1
 HALF = SLOTS // 2
+COLS = CH // 2
+PLACE = {0: 0, 1: 1, 7: 2, 2: 3, 6: 4, 3: 5, 5: 6, 4: 7}
+RUNS = ((0, 3), (3, 5))
 NIRR = 8
 
 
@@ -136,7 +139,7 @@
         rank_sub = jnp.sum(jnp.where(same & (lane_i < sub_i), 1.0, 0.0), axis=1, keepdims=True)
         return along_sub, rank_lane, rank_sub
 
-    def pack(dst):
+    def pack():
         irr_lane = jnp.sum(raw_irr[...], axis=0, keepdims=True)
         along_sub, rank_lane, _ = ranks_of(irr_lane)
         slot = lax.broadcasted_iota(jnp.int32, (SLOTS, RB), 0).astype(F32)
@@ -150,7 +153,9 @@
         packed = dot(pick, high) + dot(pick, mid) + dot(pick, low)
         last = lax.broadcasted_iota(jnp.int32, (SLOTS, CH), 0) == CAP
         tail = jnp.concatenate([irr_lane, jnp.zeros((1, CH - RB), F32)], axis=1)
-        dst[...] = jnp.where(last, jnp.broadcast_to(tail, (SLOTS, CH)), packed)
+        packed = jnp.where(last, jnp.broadcast_to(tail, (SLOTS, CH)), packed)
+        pbuf[0, y, 0] = packed[:, :COLS]
+        qbuf[0, 0, 0] = packed[:, COLS:]
 
     def open_blocks(g, srcs):
         for k, src in enumerate(srcs):
@@ -162,8 +167,10 @@
             irr_col[g, k * RB:(k + 1) * RB, :] = along_sub
             ranks[pl.ds(NX * g + k, 1), :] = rank_lane
 
-    def multiply(g, src, j, first=False):
-        high, low = split(src.reshape(NX * SLOTS, CH))
+    def multiply(g, slot, first=False):
+        j, rows = ymod(-slot), (NX * SLOTS, COLS)
+        both = jnp.concatenate([pbuf[g, j].reshape(rows), qbuf[g, :, PLACE[slot]].reshape(rows)], axis=1)
+        high, low = split(both)
         spread = dot(sel[g], jnp.concatenate([high, low], axis=1))
         keep = jnp.concatenate([irr_col[g], irr_col[g]], axis=1) == ci_ref[pl.ds(j, 1), :]
         e_hi = jnp.where(keep, spread[:, :CH], 0.0).astype(BF16)
@@ -176,77 +183,102 @@
 
     arrived(raw_irr.at[pl.ds(0, NY - 1)], ri_r.at[0])
     arrived(raw.at[pl.ds(0, NY - 1)], raw_r.at[0])
-    pack(qbuf.at[x, y])
-
-    def q_along_x(j, slot):
-        for k in (1, 3, 2):
-            send(qbuf.at[x, j], qbuf.at[x, j], qx_s.at[0], qx_r.at[slot], x_peers[k - 1])
-
-    def part(ref, half):
-        return ref if half is None else ref.at[pl.ds(half * HALF, HALF)]
-
-    def p_along_y(j, k, s, direction):
-        half = direction if s == NY // 2 else None
-        ref = part(pbuf.at[j, xmod(-k)], half)
-        send(ref, ref, py_s.at[0], py_r.at[direction, s, k], (up, down)[direction])
-
-    def q_step(k):
-        arrived(qbuf.at[x, ymod(-k)], qy_r.at[k])
-        q_along_x(ymod(-k), k)
-
-    def p_step(s, ks):
-        for k in ks:
-            for direction, j in ((0, ymod(-s)), (1, ymod(s))):
-                arrived(pbuf.at[j, xmod(-k)], py_r.at[direction, s, k])
-                p_along_y(j, k, s + 1, direction)
-
-    send(qbuf.at[x, y], pbuf.at[y, x], zx_s.at[0], zx_r.at[0], across)
-    for k in (1, 7, 2, 6, 3, 5, 4):
-        send(qbuf.at[x, y], qbuf.at[x, y], qy_s.at[0], qy_r.at[k], y_peers[k - 1])
-    q_along_x(y, 0)
+    pack()
+
+    def q_start(g):
+        for k in (1, 7, 2, 6, 3, 5, 4):
+            send(qbuf.at[g, 0, 0], qbuf.at[g, 0, PLACE[k]], qy_s.at[0], qy_r.at[g, int(PLACE[k] > 2)], y_peers[k - 1])
+
+    def q_along_x(g, run):
+        at, count = RUNS[run]
+        come = pl.ds(max(at, 1), count - (run == 0))
+        arrived(qbuf.at[g, 0, come], qy_r.at[g, run])
+        for k in (2, 1, 3):
+            send(
+                qbuf.at[g, 0, pl.ds(at, count)], qbuf.at[g, k, pl.ds(at, count)],
+                qx_s.at[0], qx_r.at[g, run], x_peers[k - 1],
+            )
+
+    def q_here(g, run):
+        at, count = RUNS[run]
+        arrived(qbuf.at[g, pl.ds(1, NX - 1), pl.ds(at, count)], qx_r.at[g, run])
+
+    def p_part(g, j, group, s, direction):
+        which = pl.ds(0, 1) if group == 0 else pl.ds(1, NX - 1)
+        if s == NY // 2:
+            return pbuf.at[g, j, which, pl.ds(direction * HALF, HALF)]
+        return pbuf.at[g, j, which]
+
+    def p_along_y(g, j, group, s, direction):
+        ref = p_part(g, j, group, s, direction)
+        send(ref, ref, py_s.at[0], py_r.at[g, direction, s, group], (up, down)[direction])
+
+    def p_start(g):
+        for k in (2, 1, 3):
+            send(pbuf.at[g, y, 0], pbuf.at[g, y, k], px_s.at[0], px_r.at[g], x_peers[k - 1])
+        for direction in (0, 1):
+            p_along_y(g, y, 0, 1, direction)
+
+    def p_x(g):
+        arrived(pbuf.at[g, y, pl.ds(1, NX - 1)], px_r.at[g])
+        for direction in (0, 1):
+            p_along_y(g, y, 1, 1, direction)
+
+    def p_step(g, s, group):
+        for direction, j in ((0, ymod(-s)), (1, ymod(s))):
+            arrived(p_part(g, j, group, s, direction), py_r.at[g, direction, s, group])
+            p_along_y(g, j, group, s + 1, direction)
 
     opposite = ymod(NY // 2)
 
-    def q_multiply(slot, first=False):
-        j = ymod(-slot)
-        arrived(qbuf.at[0, pl.ds(0, NX - 1)], qx_r.at[slot])
-        if first:
-            open_blocks(0, [qbuf.at[k, j] for k in range(NX)])
-        multiply(0, qbuf[:, j], j, first)
-
-    def p_multiply(j, first=False):
-        if first:
-            open_blocks(1, [pbuf.at[j, k] for k in range(NX)])
-        multiply(1, pbuf[j], j, first)
-
-    for k in (1, 7, 2, 6):
-        q_step(k)
-    arrived(pbuf.at[y, x], zx_r.at[0])
-    p_along_y(y, 0, 1, 0)
-    p_along_y(y, 0, 1, 1)
-    for k in (1, 3, 2):
-        send(pbuf.at[y, x], pbuf.at[y, x], px_s.at[0], px_r.at[k], x_peers[k - 1])
-    for k in (3, 5, 4):
-        q_step(k)
-    q_multiply(0, first=True)
-    p_step(1, (0,))
-    for k in (1, 3, 2):
-        arrived(pbuf.at[y, xmod(-k)], px_r.at[k])
-        p_along_y(y, k, 1, 0)
-        p_along_y(y, k, 1, 1)
-    q_multiply(1)
-    q_multiply(7)
-    p_step(1, (1, 3, 2))
-    p_multiply(y, first=True)
-    q_multiply(2)
-    q_multiply(6)
-    p_step(2, (0,))
-    q_multiply(3)
-    q_multiply(5)
-    p_step(2, (1, 3, 2))
-    q_multiply(4)
-
-    block = lambda d: pl.ds(pl.multiple_of(d * RB, RB), RB)
+    def p_last(g):
+        for group in (0, 1):
+            for direction in (0, 1):
+                arrived(p_part(g, opposite, group, NY // 2, direction), py_r.at[g, direction, NY // 2, group])
+
+    def use(g, *slots):
+        for slot in slots:
+            if slot == 0:
+                open_blocks(g, [pbuf.at[g, y, k] for k in range(NX)])
+            multiply(g, slot, slot == 0)
+
+    send(pbuf.at[0, y, 0], pbuf.at[1, y, 0], zx_s.at[0], zx_r.at[0], across)
+    send(qbuf.at[0, 0, 0], qbuf.at[1, 0, 0], zx_s.at[0], zx_r.at[1], across)
+    p_start(0)
+    q_start(0)
+    q_along_x(0, 0)
+    p_step(0, 1, 0)
+    p_x(0)
+    arrived(pbuf.at[1, y, 0], zx_r.at[0])
+    p_start(1)
+    arrived(qbuf.at[1, 0, 0], zx_r.at[1])
+    q_start(1)
+    p_step(0, 2, 0)
+    q_along_x(0, 1)
+    p_step(0, 1, 1)
+    q_here(0, 0)
+    use(0, 0)
+    p_step(0, 3, 0)
+    q_along_x(1, 0)
+    p_step(1, 1, 0)
+    p_step(0, 2, 1)
+    p_x(1)
+    use(0, 1, 7)
+    p_step(1, 2, 0)
+    q_along_x(1, 1)
+    p_step(0, 3, 1)
+    p_step(1, 1, 1)
+    q_here(0, 1)
+    use(0, 2, 6)
+    q_here(1, 0)
+    use(1, 0)
+    p_step(1, 3, 0)
+    use(0, 3, 5)
+    p_step(1, 2, 1)
+    p_last(0)
+    use(0, 4)
+
+    block = lambda d: pl.ds(pl.multiple_of(xmod(-d) * RB, RB), RB)
 
     def pair_copy(g, d):
         return pltpu.make_async_remote_copy(
@@ -293,34 +325,30 @@
         loads[2].wait()
         out_ref[...] = res_ref[...] + 0.5 * total
 
-    keeps_q = c == zh
-
-    @pl.when(jnp.logical_not(keeps_q))
+    keeps_own = c == zh
+
+    @pl.when(jnp.logical_not(keeps_own))
     def _():
         give(0)
 
-    p_multiply(ymod(-1))
-    p_multiply(ymod(1))
-
-    @pl.when(keeps_q)
+    use(1, 1, 7)
+
+    @pl.when(keeps_own)
     def _():
         take(0)
 
-    p_step(3, (0, 1, 3, 2))
-    for s in (2, 3):
-        p_multiply(ymod(-s))
-        p_multiply(ymod(s))
-    for k in (0, 1, 3, 2):
-        for direction in (0, 1):
-            arrived(part(pbuf.at[opposite, xmod(-k)], direction), py_r.at[direction, NY // 2, k])
-    p_multiply(opposite)
-
-    @pl.when(keeps_q)
+    p_step(1, 3, 1)
+    q_here(1, 1)
+    use(1, 2, 6, 3, 5)
+    p_last(1)
+    use(1, 4)
+
+    @pl.when(keeps_own)
     def _():
         give(1)
         finish(0)
 
-    @pl.when(jnp.logical_not(keeps_q))
+    @pl.when(jnp.logical_not(keeps_own))
     def _():
         take(1)
         finish(1)
@@ -328,11 +356,11 @@
     cnt_ref[0] = jnp.max(ranks[...])
     sent(raw.at[pl.ds(0, NY - 1)], raw_s.at[0])
     sent(raw_irr.at[pl.ds(0, NY - 1)], ri_s.at[0])
-    sent(qbuf.at[0, 0], zx_s.at[0])
-    sent(qbuf.at[0, pl.ds(0, NY - 1)], qy_s.at[0])
-    sent(qbuf.at[pl.ds(0, NX - 1)], qx_s.at[0])
-    sent(pbuf.at[0, pl.ds(0, NX - 1)], px_s.at[0])
-    sent(pbuf.at[pl.ds(0, NY - 1)], py_s.at[0])
+    sent(pbuf.at[0, 0, pl.ds(0, 2)], zx_s.at[0])
+    sent(qbuf.at[:, 0, pl.ds(0, NY - 1)], qy_s.at[0])
+    sent(qbuf.at[:, pl.ds(0, NX - 1)], qx_s.at[0])
+    sent(pbuf.at[:, 0, pl.ds(0, NX - 1)], px_s.at[0])
+    sent(pbuf.at[:, pl.ds(0, NY - 1)], py_s.at[0])
     sent(pair, pair_s.at[0])
     sent(zbuf.at[pl.ds(0, NZL - 1)], z_s.at[0])
 
@@ -358,8 +386,8 @@
             pltpu.VMEM((8, RB), F32),
             pltpu.VMEM((NY, RW, CH), F32),
             pltpu.VMEM((NY, RB), F32),
-            pltpu.VMEM((NX, NY, SLOTS, CH), F32),
-            pltpu.VMEM((NY, NX, SLOTS, CH), F32),
+            pltpu.VMEM((NZH, NX, NY, SLOTS, COLS), F32),
+            pltpu.VMEM((NZH, NY, NX, SLOTS, COLS), F32),
             pltpu.VMEM((NZH, NX * RB, NX * SLOTS), BF16),
             pltpu.VMEM((NZH, NX * RB, RB), F32),
             pltpu.VMEM((2 * NX, RB), F32),
@@ -367,8 +395,8 @@
             pltpu.VMEM((NZL, RB, AB), F32),
             pltpu.VMEM((NZL - 1, RB, AB), F32),
             dma((6,)), dma((1,)), dma((1,)), dma((1,)), dma((1,)),
-            dma((1,)), dma((NY,)), dma((1,)), dma((NY,)),
-            dma((1,)), dma((2, 5, NX)), dma((1,)), dma((NX,)), dma((1,)), dma((1,)),
+            dma((1,)), dma((NZH, 2)), dma((1,)), dma((NZH, 2)),
+            dma((1,)), dma((NZH, 2, 5, 2)), dma((1,)), dma((NZH,)), dma((1,)), dma((2,)),
             dma((1,)), dma((NZL,)), dma((1,)), dma((1,)),
         ],
         compiler_params=pltpu.CompilerParams(

time: 109 us -> 59 us (0.54)
  Pallas kernels: 106 us -> 56.3 us
    pallas_call x2 -> x1, Pallas kernels: 106 us -> 56.3 us  [one_pass(): pl.pallas_call(kernel, out_shape=(jax.ShapeDtypeStruct((RB, AB), F32), ja...]
where the time goes in v3:
time: 59 us; the launch traced here: 58.8 us
  Pallas kernels  56.3 us (95%)
  local copies, waits for them, and re-layouts  1.6 us (3%)
  loops' own time  0.87 us (1%)
    pallas_call x1, Pallas kernels, one_pass(): pl.pallas_call(kernel, out_shape=(jax.ShapeDtypeStruct((RB, AB), F32), ja...  56.3 us
    unnamed x11, local copies, waits for them, and re-layouts  1.6 us

profile of v3, /device:TPU:1, one launch (start us, length us, event | category | flops | bytes accessed | tf_op | source)
XLA Modules:
  0.0 58.8 jit_solution(1678720722419641123)
XLA Ops:
  0.0 0.0 copy-start.4
  0.0 0.0 copy-start.3
  0.0 0.0 copy-start
  0.0 0.9 %copy-done = f32[128,256]{1,0:T(8,128)S(1)} copy-done((f32[128,256]{1,0:T(8,128)S(1)}, f32[128,256]{1,0:T(8,128)}, u32[]{:S(2)}) %copy-start) | copy-done | bytes 131096
  0.9 0.0 copy-start.1
  0.9 0.0 copy-start.2
  0.9 56.3 %ladder.2 = (f32[128,256]{1,0:T(8,128)S(1)}, f32[1]{0:T(128)}) custom-call(f32[16,2048]{1,0:T(8,128)} %a_hbm.1, f32[2048,256]{1,0:T(8,128)} %int_hbm.1, f32[128,256]{1,0:T(8,128)S(1)} %copy-done, s32[16]{0:T(128)} %irr_hbm.1, s32[8]{0:T(128)} %sizes_hbm.1, f32[1]{0:T(128)} %constant.1.clone.1.off_hbm), custom_call_target="tpu_custom_call" | custom-call | tf_op jit(solution)/shard_map/ladder/pallas_call | solution.py:372
  57.2 0.0 copy-done.4
  57.3 0.0 copy-done.3
  57.3 0.0 copy-done.1
  57.3 0.0 copy-done.2
  57.3 0.9 %while.12 = (f32[128,256]{1,0:T(8,128)S(1)}, f32[1]{0:T(128)}, f32[1]{0:T(128)}, f32[16,2048]{1,0:T(8,128)S(1)}, f32[2048,256]{1,0:T(8,128)S(1)}, /*index=5*/s32[16]{0:T(128)S(1)}, s32[8]{0:T(128)S(1)}, f32[1]{0:T(128)}) while((f32[128,256]{1,0:T(8,128)S(1)}, f32[1]{0:T(128)}, f32[1]{0:T(128)}, f32[16,2048]{1,0:T(8,128)S(1)}, ...), condition=%wide.region_1.0_spmd, body=%wide.region_0.0_spmd | while | flops 2 | bytes 262237 | solution.py:424
  58.2 0.7 %copy.20 = f32[128,256]{1,0:T(8,128)} copy(f32[128,256]{1,0:T(8,128)S(1)} %get-tuple-element.48) | data formatting | bytes 262144
Async XLA Ops:
  0.0 57.2 %copy-start.4 = (s32[8]{0:T(128)S(1)}, s32[8]{0:T(128)}, u32[]{:S(2)}) copy-start(s32[8]{0:T(128)} %sizes_hbm.1) | copy-start | bytes 100
  0.0 57.3 %copy-start.3 = (s32[16]{0:T(128)S(1)}, s32[16]{0:T(128)}, u32[]{:S(2)}) copy-start(s32[16]{0:T(128)} %irr_hbm.1) | copy-start | bytes 196
  0.0 0.9 %copy-start = (f32[128,256]{1,0:T(8,128)S(1)}, f32[128,256]{1,0:T(8,128)}, u32[]{:S(2)}) copy-start(f32[128,256]{1,0:T(8,128)} %res_hbm.1) | copy-start | bytes 393220
  0.9 56.3 %copy-start.1 = (f32[2048,256]{1,0:T(8,128)S(1)}, f32[2048,256]{1,0:T(8,128)}, u32[]{:S(2)}) copy-start(f32[2048,256]{1,0:T(8,128)} %int_hbm.1) | copy-start | bytes 6291460
  0.9 56.3 %copy-start.2 = (f32[16,2048]{1,0:T(8,128)S(1)}, f32[16,2048]{1,0:T(8,128)}, u32[]{:S(2)}) copy-start(f32[16,2048]{1,0:T(8,128)} %a_hbm.1) | copy-start | bytes 393220

commit v4 on v3

--- a/solution.py
+++ b/solution.py
@@ -331,11 +331,11 @@
     def _():
         give(0)
 
-    use(1, 1, 7)
-
     @pl.when(keeps_own)
     def _():
         take(0)
+
+    use(1, 1, 7)
 
     p_step(1, 3, 1)
     q_here(1, 1)

time: 59 us -> 58.6 us (level)
  no operation moved by 1% of the time
where the time goes in v4:
time: 58.6 us; the launch traced here: 58.5 us
  Pallas kernels  56 us (96%)
  local copies, waits for them, and re-layouts  1.6 us (3%)
  loops' own time  0.87 us (1%)
    pallas_call x1, Pallas kernels, one_pass(): pl.pallas_call(kernel, out_shape=(jax.ShapeDtypeStruct((RB, AB), F32), ja...  56 us
    unnamed x11, local copies, waits for them, and re-layouts  1.6 us

profile of v4, /device:TPU:1, one launch (start us, length us, event | category | flops | bytes accessed | tf_op | source)
XLA Modules:
  0.0 58.5 jit_solution(1180633884330956939)
XLA Ops:
  0.0 0.0 copy-start.4
  0.0 0.0 copy-start.3
  0.0 0.0 copy-start
  0.0 0.9 %copy-done = f32[128,256]{1,0:T(8,128)S(1)} copy-done((f32[128,256]{1,0:T(8,128)S(1)}, f32[128,256]{1,0:T(8,128)}, u32[]{:S(2)}) %copy-start) | copy-done | bytes 131096
  0.9 0.0 copy-start.1
  0.9 0.0 copy-start.2
  0.9 56.0 %ladder.2 = (f32[128,256]{1,0:T(8,128)S(1)}, f32[1]{0:T(128)}) custom-call(f32[16,2048]{1,0:T(8,128)} %a_hbm.1, f32[2048,256]{1,0:T(8,128)} %int_hbm.1, f32[128,256]{1,0:T(8,128)S(1)} %copy-done, s32[16]{0:T(128)} %irr_hbm.1, s32[8]{0:T(128)} %sizes_hbm.1, f32[1]{0:T(128)} %constant.1.clone.1.off_hbm), custom_call_target="tpu_custom_call" | custom-call | tf_op jit(solution)/shard_map/ladder/pallas_call | solution.py:372
  56.9 0.0 copy-done.4
  56.9 0.0 copy-done.3
  56.9 0.0 copy-done.1
  56.9 0.0 copy-done.2
  56.9 0.9 %while.12 = (f32[128,256]{1,0:T(8,128)S(1)}, f32[1]{0:T(128)}, f32[1]{0:T(128)}, f32[16,2048]{1,0:T(8,128)S(1)}, f32[2048,256]{1,0:T(8,128)S(1)}, /*index=5*/s32[16]{0:T(128)S(1)}, s32[8]{0:T(128)S(1)}, f32[1]{0:T(128)}) while((f32[128,256]{1,0:T(8,128)S(1)}, f32[1]{0:T(128)}, f32[1]{0:T(128)}, f32[16,2048]{1,0:T(8,128)S(1)}, ...), condition=%wide.region_1.0_spmd, body=%wide.region_0.0_spmd | while | flops 2 | bytes 262237 | solution.py:424
  57.8 0.7 %copy.20 = f32[128,256]{1,0:T(8,128)} copy(f32[128,256]{1,0:T(8,128)S(1)} %get-tuple-element.48) | data formatting | bytes 262144
Async XLA Ops:
  0.0 56.9 %copy-start.4 = (s32[8]{0:T(128)S(1)}, s32[8]{0:T(128)}, u32[]{:S(2)}) copy-start(s32[8]{0:T(128)} %sizes_hbm.1) | copy-start | bytes 100
  0.0 56.9 %copy-start.3 = (s32[16]{0:T(128)S(1)}, s32[16]{0:T(128)}, u32[]{:S(2)}) copy-start(s32[16]{0:T(128)} %irr_hbm.1) | copy-start | bytes 196
  0.0 0.9 %copy-start = (f32[128,256]{1,0:T(8,128)S(1)}, f32[128,256]{1,0:T(8,128)}, u32[]{:S(2)}) copy-start(f32[128,256]{1,0:T(8,128)} %res_hbm.1) | copy-start | bytes 393220
  0.9 56.0 %copy-start.1 = (f32[2048,256]{1,0:T(8,128)S(1)}, f32[2048,256]{1,0:T(8,128)}, u32[]{:S(2)}) copy-start(f32[2048,256]{1,0:T(8,128)} %int_hbm.1) | copy-start | bytes 6291460
  0.9 56.0 %copy-start.2 = (f32[16,2048]{1,0:T(8,128)S(1)}, f32[16,2048]{1,0:T(8,128)}, u32[]{:S(2)}) copy-start(f32[16,2048]{1,0:T(8,128)} %a_hbm.1) | copy-start | bytes 393220
